TPU v7x, 512 devices: a whole 4x4x16 slice. The times are simulated.
512 devices in a mesh: dof: 32 (over z_lo, x), azi: 16 (over z_hi, y, core).
Axes of the slice: x: 4, y: 4, z: 16 (z_hi: 2, z_lo: 8; z = z_hi * 8 + z_lo), core: 2. Of those that a mesh axis runs over, the one named last changes fastest.
Arguments:
- forcing: bfloat16 [16, 256, 32768], P(None, 'azi', 'dof'), may hold values from -6 to 6
- mode_shapes: bfloat16 [32768, 2048], P('dof'), may hold values from -0.0625 to 0.0625
- inverses: bfloat16 [128, 32, 2, 64, 64], P('azi', 'dof'), may hold values from -0.5 to 0.5
- harmonic_table: int32 [128], replicated, may hold values from 0 to 127, each once
Outputs:
- displacement: bfloat16 [16, 256, 32768], P(None, 'azi', 'dof')
Inputs may be any that keep to these rules, and one draw needn't show every extreme that they name: `harmonic_table`: each harmonic number appears in exactly one slot; the slots are split over azi in order.
All inputs are finite; a program needn't handle non-finite values.
Results may differ from a plain program's by a relative error of at most 0.0049.
Values may be sent and summed in bfloat16 or wider, within the bound.
A program may use at most 64 MiB of HBM per device.

v0:
```python
import math

import jax
import jax.numpy as jnp
from jax import lax
from jax.sharding import PartitionSpec as P


def forward_table(harmonics, samples, length):
    angles = (samples[:, None] * harmonics[None, :] % length).astype(jnp.float32) * (
        2.0 * math.pi / length
    )
    return jnp.stack([jnp.cos(angles), -jnp.sin(angles)], axis=2).reshape(samples.shape[0], -1)


def inverse_table(harmonics, samples, length):
    angles = (harmonics[:, None] * samples[None, :] % length).astype(jnp.float32) * (
        2.0 * math.pi / length
    )
    weight = jnp.where(harmonics == 0, 1.0, 2.0).astype(jnp.float32) / length
    stacked = jnp.stack(
        [weight[:, None] * jnp.cos(angles), -weight[:, None] * jnp.sin(angles)], axis=1
    )
    return stacked.reshape(-1, samples.shape[0])


def contract(left, right):
    return jnp.einsum("sfik,fkcs->fics", left, right, precision=lax.Precision.HIGHEST)


def solve_modal(spectra, inverses):
    slot_count, families, _, family_size, _ = inverses.shape
    case_count = spectra.shape[1]
    pieces = spectra.reshape(families, family_size, case_count, slot_count, 2)
    real_in = pieces[..., 0]
    imag_in = pieces[..., 1]
    blocks = inverses.astype(jnp.float32)
    real_mat = blocks[:, :, 0]
    imag_mat = blocks[:, :, 1]
    real_out = contract(real_mat, real_in) - contract(imag_mat, imag_in)
    imag_out = contract(real_mat, imag_in) + contract(imag_mat, real_in)
    return jnp.stack([real_out, imag_out], axis=4).reshape(
        families * family_size, case_count, slot_count * 2
    )


def shards(forcing, mode_shapes, inverses, harmonic_table):
    case_count, local_samples, dof_local = forcing.shape
    sample_count = local_samples * lax.axis_size("azi")
    slot_count = inverses.shape[0]
    row_block = forcing.reshape(case_count * local_samples, dof_local)
    columns = mode_shapes
    modal_force = lax.psum_scatter(
        lax.dot_general(
            columns, row_block, (((0,), (1,)), ((), ())), preferred_element_type=jnp.float32
        ),
        "dof",
        scatter_dimension=0,
        tiled=True,
    )
    mode_local = modal_force.shape[0]
    modal_force = modal_force.reshape(mode_local, case_count, local_samples)
    all_samples = jnp.arange(sample_count, dtype=jnp.int32)
    own_samples = lax.axis_index("azi") * local_samples + jnp.arange(local_samples, dtype=jnp.int32)
    own_slots = lax.dynamic_slice_in_dim(
        harmonic_table, lax.axis_index("azi") * slot_count, slot_count
    )
    forward_part = jnp.dot(
        modal_force.reshape(-1, local_samples),
        forward_table(harmonic_table, own_samples, sample_count),
        preferred_element_type=jnp.float32,
        precision=lax.Precision.HIGHEST,
    )
    forward_part = forward_part.reshape(1, mode_local, case_count, -1)
    received = lax.all_to_all(forward_part, "azi", split_axis=3, concat_axis=0, tiled=True)
    spectra = jnp.sum(received, axis=0)
    response = solve_modal(spectra, inverses)
    back_part = jnp.dot(
        response.reshape(-1, 2 * slot_count),
        inverse_table(own_slots, all_samples, sample_count),
        preferred_element_type=jnp.float32,
        precision=lax.Precision.HIGHEST,
    )
    back_part = back_part.reshape(1, mode_local, case_count, sample_count)
    returned = lax.all_to_all(back_part, "azi", split_axis=3, concat_axis=0, tiled=True)
    modal_coords = jnp.sum(returned, axis=0)
    modal_coords = modal_coords.astype(jnp.bfloat16).reshape(mode_local, case_count * local_samples)
    columns = mode_shapes
    displaced = lax.dot_general(
        lax.all_gather(modal_coords, "dof", axis=0, tiled=True),
        columns,
        (((0,), (1,)), ((), ())),
        preferred_element_type=jnp.float32,
    )
    return displaced.reshape(case_count, local_samples, dof_local).astype(jnp.bfloat16)


def solution(mesh):
    in_specs = (P(None, "azi", "dof"), P("dof", None), P("azi", "dof", None, None, None), P())
    out_specs = P(None, "azi", "dof")
    return jax.shard_map(shards, mesh=mesh, in_specs=in_specs, out_specs=out_specs, check_vma=False)
```

profile of v0, /device:TPU:6, one launch (start us, length us, event | category | flops | bytes accessed | tf_op | source)
XLA Modules:
  0.0 595.8 jit_solution(7525761207662108501)
XLA Ops:
  6.5 1.0 copy-done
  7.6 4.9 fusion.24
  12.5 0.1 fusion.21
  12.8 246.9 %reduce-scatter.2.cloned.1.call-done = f32[64,256]{1,0:T(8,128)} async-done(((f32[2048,256]{1,0:T(8,128)}), f32[64,256]{1,0:T(8,128)}) %reduce-scatter.2.cloned.1.call-update) | async-done | bytes 65552 | tf_op jit(solution)/shard_map/reduce_scatter | solution.py:53
  259.7 0.9 copy.66
  260.6 0.3 copy.68
  260.9 2.0 convolution_bitcast_fusion.1
  262.9 2.7 copy.70
  265.6 2.3 reshape.343
  267.9 9.7 %all-to-all-start = ((f32[16,1,16384]{2,1,0:T(1,128)}), f32[16,1,16384]{2,1,0:T(1,128)S(1)}, u32[]{:S(2)}, u32[]{:S(2)}) async-start(f32[16,1,16384]{2,1,0:T(1,128)} %reshape.343), calls=%async_computation.1 | async-start | bytes 2097152 | tf_op jit(solution)/shard_map/all_to_all | solution.py:75
  277.6 0.2 all-gather.2.cloned.1.call-start
  278.0 0.1 cosine_multiply_fusion
  278.1 28.4 %all-to-all-done = f32[16,1,16384]{2,1,0:T(1,128)S(1)} async-done(((f32[16,1,16384]{2,1,0:T(1,128)}), f32[16,1,16384]{2,1,0:T(1,128)S(1)}, u32[]{:S(2)}, u32[]{:S(2)}) %all-to-all-start) | async-done | bytes 1048608 | tf_op jit(solution)/shard_map/all_to_all | solution.py:75
  306.5 0.5 broadcast.300
  307.0 4.4 reduce.8
  311.4 2.1 reshape.344
  313.5 0.2 reduce.6
  313.7 0.3 fusion.4
  314.0 0.3 fusion.6
  314.3 0.3 fusion
  314.6 0.3 fusion.1
  315.0 0.3 copy.79
  315.3 1.9 convolution_bitcast_fusion
  317.2 2.7 copy.80
  320.0 2.3 reshape.345
  322.3 36.8 %all_to_all.24 = f32[16,1,16384]{2,1,0:T(1,128)S(1)} all-to-all(f32[16,1,16384]{2,1,0:T(1,128)} %reshape.345), channel_id=1, replica_groups=mesh['dof'=32,'azi'=16] {'azi'}, dimensions={0} | all-to-all | bytes 2097152 | tf_op jit(solution)/shard_map/all_to_all | solution.py:85
  359.0 4.4 reduce.9
  363.4 2.1 reshape.346
  365.5 0.2 reduce.7
  365.7 0.7 copy.82
  366.4 217.9 %all-gather.2.cloned.1.call-done = bf16[2048,256]{1,0:T(8,128)(2,1)} async-done(((bf16[64,256]{1,0:T(8,128)(2,1)}), bf16[2048,256]{1,0:T(8,128)(2,1)}) %all-gather.2.cloned.1.call-update) | async-done | bytes 1048592 | tf_op jit(solution)/shard_map/all_gather | solution.py:90
  584.4 4.6 convolution_convert_fusion
  (19 shorter events, 0.3 us)
Async XLA Ops:
  6.5 1.0 copy-start
  6.5 253.1 %reduce-scatter.2.cloned.1.call-start = ((), (), s32[]{:S(2)}) async-start(), calls=%async_computation.3 | async-start | bytes 2162688 | tf_op jit(solution)/shard_map/reduce_scatter | solution.py:53
  7.6 4.9 copy-start.2
  267.9 38.6 %all-to-all-start = ((f32[16,1,16384]{2,1,0:T(1,128)}), f32[16,1,16384]{2,1,0:T(1,128)S(1)}, u32[]{:S(2)}, u32[]{:S(2)}) async-start(f32[16,1,16384]{2,1,0:T(1,128)} %reshape.343), calls=%async_computation.1 | async-start | bytes 2097152 | tf_op jit(solution)/shard_map/all_to_all | solution.py:75
  277.6 36.0 %copy-start.1 = (bf16[8,1,2,64,64]{4,3,2,1,0:T(8,128)(2,1)S(1)}, bf16[8,1,2,64,64]{4,3,2,1,0:T(8,128)(2,1)}, u32[]{:S(2)}) copy-start(bf16[8,1,2,64,64]{4,3,2,1,0:T(8,128)(2,1)} %param.6) | copy-start | bytes 393220
  277.6 306.7 %all-gather.2.cloned.1.call-start = ((), (), s32[]{:S(2)}) async-start(), calls=%async_computation.4 | async-start | bytes 1081344 | tf_op jit(solution)/shard_map/all_gather | solution.py:90
Sparse Core Ops, SparseCore 0:
  12.6 247.0 reduce-scatter.1
  366.5 217.7 all-gather.1
where the time goes:
time: 606 us; the launch traced here: 596 us
  waiting for transfers between devices  493 us (81%)
  blocking collectives  36.8 us (6%)
  local copies, waits for them, and re-layouts  18.1 us (3%)
  matrix products  14.7 us (2%)
  between operations  13.6 us (2%)
  starting transfers between devices  9.95 us (2%)
  other arithmetic  9.51 us (2%)
    reduce_scatter x1, waiting for transfers between devices, shards(): lax.psum_scatter(lax.dot_general(columns, row_block, (((0,), (1,)), ((),...  247 us
    all_gather x1, waiting for transfers between devices, shards(): lax.all_gather(modal_coords, 'dof', axis=0, tiled=True)  218 us
    all_to_all x1, blocking collectives, shards(): lax.all_to_all(back_part, 'azi', split_axis=3, concat_axis=0, tiled=True)  36.8 us
    all_to_all x1, waiting for transfers between devices, shards(): lax.all_to_all(forward_part, 'azi', split_axis=3, concat_axis=0, tiled=True)  28.4 us
  transfers between devices with their start and end apart: 3, of which 3 were waited for; matrix products, arithmetic and copies ran while one was open for 0% of the time, Pallas kernels for 0%

commit v1 on v0

v1 whole, which is shorter than its diff:
```python
import functools
import math

import jax
import jax.numpy as jnp
from jax import lax
from jax.experimental import pallas as pl
from jax.experimental.pallas import tpu as pltpu
from jax.sharding import PartitionSpec as P

BF16 = jnp.bfloat16
F32 = jnp.float32
MESH = pl.DeviceIdType.MESH

DIMS = dict(Z=8, X=4, H=2, Y=4)


def kernel(
    Z, X, H, Y,
    f_hbm, s_hbm, inv_hbm, harm_hbm, out_hbm,
    f_v, s_v, inv_v, harm_v, pbuf, sendx, recvx, sendz, recvz,
    t_hi, t_lo, u_hi, u_lo, fwd, bwd, amat, xg, rg, qacc, cacc, coords, acc, out_v,
    f_sem, s_sem, i_sem, h_sem, o_sem,
    sx_sem, rx_sem, sz_sem, rz_sem, sg_sem, rg_sem, sr_sem, rr_sem,
    scz_sem, rcz_sem, scx_sem, rcx_sem,
):
    fam = inv_v.shape[2]
    slots = inv_v.shape[0]
    cases, own_t, depth = f_v.shape
    ct = cases * own_t
    azis = H * Y * 2
    length = azis * own_t
    nh = harm_v.shape[1]
    gathered = azis

    dof = lax.axis_index("dof")
    azi = lax.axis_index("azi")
    x = dof % X
    z = dof // X
    core = azi % 2
    y = (azi // 2) % Y
    h = azi // (2 * Y)

    def x_peer(r):
        return {"dof": z * X + (x + r) % X, "azi": azi}

    def z_peer(r):
        return {"dof": ((z + r) % Z) * X + x, "azi": azi}

    def y_peer(r):
        return {"dof": dof, "azi": (h * Y + (y + r) % Y) * 2 + core}

    def h_peer():
        return {"dof": dof, "azi": ((1 - h) * Y + y) * 2 + core}

    def c_peer():
        return {"dof": dof, "azi": (h * Y + y) * 2 + 1 - core}

    peers = [x_peer(r) for r in range(1, X)] + [z_peer(r) for r in range(1, Z)]
    peers += [y_peer(r) for r in range(1, Y)] + ([h_peer()] if H > 1 else []) + [c_peer()]

    barrier = pltpu.get_barrier_semaphore()
    for peer in peers:
        pl.semaphore_signal(barrier, inc=1, device_id=peer, device_id_type=MESH)

    def remote(src, dst, send, recv, peer):
        return pltpu.make_async_remote_copy(
            src_ref=src, dst_ref=dst, send_sem=send, recv_sem=recv,
            device_id=peer, device_id_type=MESH,
        )

    def f_copy():
        return pltpu.make_async_copy(f_hbm, f_v, f_sem)

    def s_copy(k):
        target = (z + 1 + k) % Z
        columns = pl.ds(pl.multiple_of(target * (X * fam), X * fam), X * fam)
        return pltpu.make_async_copy(s_hbm.at[:, columns], s_v.at[k], s_sem.at[k])

    def i_copy():
        return pltpu.make_async_copy(inv_hbm, inv_v, i_sem)

    def h_copy():
        return pltpu.make_async_copy(harm_hbm, harm_v, h_sem)

    f_copy().start()
    for k in range(Z):
        s_copy(k).start()
    h_copy().start()
    i_copy().start()
    f_copy().wait()

    def x_copy(k, r):
        rows = pl.ds(pl.multiple_of(((x + r) % X) * fam, fam), fam)
        return remote(
            sendx.at[k, rows], recvx.at[k, r - 1], sx_sem.at[k, r - 1], rx_sem.at[k, r - 1], x_peer(r)
        )

    def multiply(k):
        s_copy(k).wait()
        part = jnp.dot(f_v[...].reshape(ct, depth), s_v[k], preferred_element_type=F32)
        part = part.T
        pbuf[k] = part
        sendx[k] = part.astype(BF16)

    multiply(0)
    pl.semaphore_wait(barrier, len(peers))
    for r in range(1, X):
        x_copy(0, r).start()

    def multiply_send(k, carry):
        multiply(k)
        for r in range(1, X):
            x_copy(k, r).start()
        return carry

    lax.fori_loop(1, Z, multiply_send, 0)

    own_rows = pl.ds(pl.multiple_of(x * fam, fam), fam)

    def z_copy(k):
        return remote(sendz.at[k], recvz.at[k], sz_sem.at[k], rz_sem.at[k], z_peer(1 + k))

    def x_sum(k):
        total = pbuf[k, own_rows]
        for r in range(1, X):
            x_copy(k, r).wait_recv()
            total += recvx[k, r - 1].astype(F32)
        return total

    def x_reduce(k, carry):
        sendz[k] = x_sum(k).astype(BF16)
        z_copy(k).start()
        return carry

    lax.fori_loop(0, Z - 1, x_reduce, 0)

    h_copy().wait()
    i_copy().wait()

    harm = jnp.broadcast_to(harm_v[...].astype(F32).astype(BF16), (ct, nh))
    column = lax.broadcasted_iota(jnp.int32, (ct, nh), 0)
    lane = lax.broadcasted_iota(jnp.int32, (ct, nh), 1)
    pick = jnp.where(lane == azi * slots + column % slots, 1.0, 0.0).astype(BF16)
    lanes = (((1,), (1,)), ((), ()))
    rows_t = lax.broadcasted_iota(jnp.int32, (length, ct), 0)
    cols_t = lax.broadcasted_iota(jnp.int32, (length, ct), 1)

    def cosine(index):
        return jnp.cos(index.astype(F32) * (2.0 * math.pi / length))

    def split(value):
        high = value.astype(BF16)
        return high, (value - high.astype(F32)).astype(BF16)

    harm_rows = jnp.broadcast_to(harm_v[...].astype(F32).astype(BF16), (length, nh))
    own_h = lax.dot_general(harm_rows, pick, lanes, preferred_element_type=F32).astype(jnp.int32)
    quarter = length // 4
    part_t = (cols_t // slots) % 2
    table = cosine((own_h * rows_t + part_t * quarter) % length)
    t_hi[...], t_lo[...] = split(table)

    row_s = lax.broadcasted_iota(jnp.int32, (length, nh), 0)
    lane_s = lax.broadcasted_iota(jnp.int32, (length, nh), 1)
    pick_rows = jnp.where(
        lane_s == (row_s // (2 * slots)) * slots + row_s % slots, 1.0, 0.0
    ).astype(BF16)
    all_h = lax.dot_general(pick_rows, harm, lanes, preferred_element_type=F32).astype(jnp.int32)
    sample = azi * own_t + cols_t % own_t
    part_u = (rows_t // slots) % 2
    weight = jnp.where(all_h == 0, 1.0 / length, 2.0 / length)
    table = weight * cosine((all_h * sample + part_u * quarter) % length)
    u_hi[...], u_lo[...] = split(table)

    row_c = lax.broadcasted_iota(jnp.int32, (ct, ct), 0) // own_t
    col_c = lax.broadcasted_iota(jnp.int32, (ct, ct), 1) // own_t
    same = jnp.where(row_c == col_c, 1.0, 0.0).astype(BF16)

    def owner(slot):
        dc = slot % 2
        dy = (slot // 2) % Y
        dh = slot // (2 * Y)
        return ((h + dh) % H * Y + (y - dy + Y) % Y) * 2 + (core + dc) % 2

    def spread(ref, slot):
        rows = pl.ds(pl.multiple_of(owner(slot) * own_t, own_t), own_t)
        block = ref[rows]
        wide = jnp.broadcast_to(block[None], (cases, own_t, ct)).reshape(ct, ct)
        return wide * same

    def build_fwd(slot, carry):
        fwd[slot, 0] = spread(t_hi, slot)
        fwd[slot, 1] = spread(t_lo, slot)
        return carry

    lax.fori_loop(0, gathered, build_fwd, 0)

    total = x_sum(Z - 1)
    for k in range(Z - 1):
        z_copy(k).wait_recv()
        total += recvz[k].astype(F32)
    xg[0] = total.astype(BF16)

    def gather(buf, send, recv, consume, between):
        def slot(dh, dy, dc):
            return (dh * Y + dy) * 2 + dc

        def to_y(dh, r):
            src, dst = slot(dh, 0, 0), slot(dh, r, 0)
            return remote(buf.at[src], buf.at[dst], send.at[dst], recv.at[dst], y_peer(r))

        def to_h():
            src, dst = slot(0, 0, 0), slot(1, 0, 0)
            return remote(buf.at[src], buf.at[dst], send.at[dst], recv.at[dst], h_peer())

        def to_c(dh, dy):
            src, dst = slot(dh, dy, 0), slot(dh, dy, 1)
            return remote(buf.at[src], buf.at[dst], send.at[dst], recv.at[dst], c_peer())

        ring = [1, 3, 2] if Y == 4 else list(range(1, Y))
        if H > 1:
            to_h().start()
        for r in ring:
            to_y(0, r).start()
        to_c(0, 0).start()
        between()
        consume(slot(0, 0, 0))
        for r in ring:
            to_y(0, r).wait_recv()
            to_c(0, r).start()
        if H > 1:
            to_h().wait_recv()
            for r in ring:
                to_y(1, r).start()
            to_c(1, 0).start()
        for r in ring:
            consume(slot(0, r, 0))
        for dy in [0] + ring:
            to_c(0, dy).wait_recv()
            consume(slot(0, dy, 1))
        if H > 1:
            consume(slot(1, 0, 0))
            for r in ring:
                to_y(1, r).wait_recv()
                to_c(1, r).start()
                consume(slot(1, r, 0))
            for dy in [0] + ring:
                to_c(1, dy).wait_recv()
                consume(slot(1, dy, 1))
        for dh in range(H):
            for r in ring:
                to_y(dh, r).wait_send()
            for dy in range(Y):
                to_c(dh, dy).wait_send()
        if H > 1:
            to_h().wait_send()

    def build_bwd(slot, carry):
        bwd[slot, 0] = spread(u_hi, slot)
        bwd[slot, 1] = spread(u_lo, slot)
        return carry

    def prepare():
        for s in range(slots):
            amat[s * fam:(s + 1) * fam, 0:fam] = inv_v[s, 0]
            amat[s * fam:(s + 1) * fam, fam:2 * fam] = inv_v[s, 1]
        lax.fori_loop(0, gathered, build_bwd, 0)

    qacc[...] = jnp.zeros_like(qacc)

    def forward(slot):
        block = xg[slot]
        qacc[...] += (
            jnp.dot(block, fwd[slot, 0], preferred_element_type=F32)
            + jnp.dot(block, fwd[slot, 1], preferred_element_type=F32)
        )

    gather(xg, sg_sem, rg_sem, forward, prepare)

    q = qacc[...]
    cols = lax.broadcasted_iota(jnp.int32, (fam, ct), 1)
    turned = jnp.where(
        (cols // slots) % 2 == 0, -pltpu.roll(q, ct - slots, 1), pltpu.roll(q, slots, 1)
    )
    q_hi, q_lo = split(jnp.concatenate([q, turned], axis=0))
    solved = jnp.dot(amat[...], q_hi, preferred_element_type=F32)
    solved += jnp.dot(amat[...], q_lo, preferred_element_type=F32)
    response = jnp.zeros((fam, ct), F32)
    for s in range(slots):
        response = jnp.where(cols % slots == s, solved[s * fam:(s + 1) * fam], response)
    rg[0] = response.astype(BF16)

    cacc[...] = jnp.zeros_like(cacc)

    def backward(slot):
        block = rg[slot]
        cacc[...] += (
            jnp.dot(block, bwd[slot, 0], preferred_element_type=F32)
            + jnp.dot(block, bwd[slot, 1], preferred_element_type=F32)
        )

    gather(rg, sr_sem, rr_sem, backward, lambda: None)

    coords[0, own_rows] = cacc[...].astype(BF16)

    def c_to_z(r):
        return remote(
            coords.at[0, own_rows], coords.at[r, own_rows], scz_sem.at[r - 1], rcz_sem.at[r - 1], z_peer(r)
        )

    def c_to_x(r, q):
        return remote(
            coords.at[r, own_rows], coords.at[r, own_rows],
            scx_sem.at[r, q - 1], rcx_sem.at[r, q - 1], x_peer(q),
        )

    def c_from_x(r, q):
        rows = pl.ds(pl.multiple_of(((x - q + X) % X) * fam, fam), fam)
        return remote(
            coords.at[r, rows], coords.at[r, rows],
            scx_sem.at[r, q - 1], rcx_sem.at[r, q - 1], x_peer(q),
        )

    for q in range(1, X):
        c_to_x(0, q).start()
    for r in range(1, Z):
        c_to_z(r).start()

    acc[...] = jnp.zeros_like(acc)

    def displace(r):
        for q in range(1, X):
            c_from_x(r, q).wait_recv()
        block = coords[r].astype(F32).T.astype(BF16)
        acc[...] += lax.dot_general(block, s_v[Z - 1 - r], lanes, preferred_element_type=F32)

    def spread_displace(r, carry):
        c_to_z(r).wait_recv()
        for q in range(1, X):
            c_to_x(r, q).start()
        displace(r - 1)
        return carry

    lax.fori_loop(1, Z, spread_displace, 0)
    displace(Z - 1)

    out_v[...] = acc[...].astype(BF16).reshape(cases, own_t, depth)
    out_copy = pltpu.make_async_copy(out_v, out_hbm, o_sem)
    out_copy.start()

    def drain_x(k, carry):
        for r in range(1, X):
            x_copy(k, r).wait_send()
            c_to_x(k, r).wait_send()
        return carry

    lax.fori_loop(0, Z, drain_x, 0)
    for k in range(Z - 1):
        z_copy(k).wait_send()
        c_to_z(k + 1).wait_send()
    out_copy.wait()


def shards(dims, forcing, mode_shapes, inverses, harmonic_table):
    Z, X, H, Y = dims["Z"], dims["X"], dims["H"], dims["Y"]
    cases, own_t, depth = forcing.shape
    slots, _, _, fam, _ = inverses.shape
    ct = cases * own_t
    azis = H * Y * 2
    length = azis * own_t
    nh = harmonic_table.shape[0]
    any_space = pl.BlockSpec(memory_space=pl.ANY)
    dma = pltpu.SemaphoreType.DMA
    zs, xs = max(Z - 1, 1), max(X - 1, 1)
    return pl.pallas_call(
        functools.partial(kernel, Z, X, H, Y),
        out_shape=jax.ShapeDtypeStruct(forcing.shape, BF16),
        in_specs=[any_space] * 4,
        out_specs=any_space,
        scratch_shapes=[
            pltpu.VMEM((cases, own_t, depth), BF16),
            pltpu.VMEM((Z, depth, X * fam), BF16),
            pltpu.VMEM((slots, 2, fam, fam), BF16),
            pltpu.VMEM((1, nh), jnp.int32),
            pltpu.VMEM((Z, X * fam, ct), F32),
            pltpu.VMEM((Z, X * fam, ct), BF16),
            pltpu.VMEM((Z, xs, fam, ct), BF16),
            pltpu.VMEM((zs, fam, ct), BF16),
            pltpu.VMEM((zs, fam, ct), BF16),
            pltpu.VMEM((length, ct), BF16),
            pltpu.VMEM((length, ct), BF16),
            pltpu.VMEM((length, ct), BF16),
            pltpu.VMEM((length, ct), BF16),
            pltpu.VMEM((azis, 2, ct, ct), BF16),
            pltpu.VMEM((azis, 2, ct, ct), BF16),
            pltpu.VMEM((slots * fam, 2 * fam), BF16),
            pltpu.VMEM((azis, fam, ct), BF16),
            pltpu.VMEM((azis, fam, ct), BF16),
            pltpu.VMEM((fam, ct), F32),
            pltpu.VMEM((fam, ct), F32),
            pltpu.VMEM((Z, X * fam, ct), BF16),
            pltpu.VMEM((ct, depth), F32),
            pltpu.VMEM((cases, own_t, depth), BF16),
            dma, dma((Z,)), dma, dma, dma,
            dma((Z, xs)), dma((Z, xs)), dma((zs,)), dma((zs,)),
            dma((azis,)), dma((azis,)), dma((azis,)), dma((azis,)),
            dma((zs,)), dma((zs,)), dma((Z, xs)), dma((Z, xs)),
        ],
        compiler_params=pltpu.CompilerParams(
            collective_id=0, has_side_effects=True, vmem_limit_bytes=48 * 1024 * 1024
        ),
        name="forced_response",
    )(
        forcing,
        mode_shapes,
        inverses.reshape(slots, 2, fam, fam),
        harmonic_table.reshape(1, nh),
    )


def solution(mesh, dims=DIMS):
    in_specs = (P(None, "azi", "dof"), P("dof", None), P("azi", "dof", None, None, None), P())
    out_specs = P(None, "azi", "dof")
    return jax.shard_map(
        functools.partial(shards, dims), mesh=mesh, in_specs=in_specs, out_specs=out_specs, check_vma=False
    )
```

time: 606 us -> 94.1 us (0.16); the launches traced: 596 us -> 92.4 us
  waiting for transfers between devices: 493 us -> 0 us
  Pallas kernels: 0 us -> 86.7 us
  blocking collectives: 36.8 us -> 0 us
  matrix products: 14.7 us -> 0 us
  between operations: 13.6 us -> 0.01 us
  local copies, waits for them, and re-layouts: 18.1 us -> 5.63 us
  starting transfers between devices: 9.95 us -> 0 us
  other arithmetic: 9.51 us -> 0 us
    reduce_scatter x1 -> x0, waiting for transfers between devices: 247 us -> none  [shards(): lax.psum_scatter(lax.dot_general(columns, row_block, (((0,), (1,)), ((),...]
    all_gather x1 -> x0, waiting for transfers between devices: 218 us -> none  [shards(): lax.all_gather(modal_coords, 'dof', axis=0, tiled=True)]
    pallas_call x0 -> x1, Pallas kernels: none -> 86.7 us  [shards(): pl.pallas_call(functools.partial(kernel, Z, X, H, Y), out_shape=jax.Shape...]
    all_to_all x1 -> x0, blocking collectives: 36.8 us -> none  [shards(): lax.all_to_all(back_part, 'azi', split_axis=3, concat_axis=0, tiled=True)]
    all_to_all x1 -> x0, waiting for transfers between devices: 28.4 us -> none  [shards(): lax.all_to_all(forward_part, 'azi', split_axis=3, concat_axis=0, tiled=True)]
    dot_general x8 -> x0, matrix products: 14.7 us -> none  [the longest x1 4.89 us: shards(): lax.dot_general(columns, row_block, (((0,), (1,)), ((), ())), preferred_e...]
    all_to_all x1 -> x0, starting transfers between devices: 9.73 us -> none  [shards(): lax.all_to_all(forward_part, 'azi', split_axis=3, concat_axis=0, tiled=True)]
    all_to_all x2 -> x0, other arithmetic: 8.82 us -> none  [the longest x1 4.41 us: shards(): lax.all_to_all(back_part, 'azi', split_axis=3, concat_axis=0, tiled=True)]
  transfers between devices with their start and end apart: 3 -> 0, of which waited for: 3 -> 0; matrix products, arithmetic and copies ran while one was open for 0% -> 0% of each run, Pallas kernels for 0% -> 0%
where the time goes in v1:
time: 94.1 us; the launch traced here: 92.4 us
  Pallas kernels  86.7 us (92%)
  local copies, waits for them, and re-layouts  5.63 us (6%)
    pallas_call x1, Pallas kernels, shards(): pl.pallas_call(functools.partial(kernel, Z, X, H, Y), out_shape=jax.Shape...  86.7 us
    unnamed x9, local copies, waits for them, and re-layouts  5.63 us

profile of v1, /device:TPU:6, one launch (start us, length us, event | category | flops | bytes accessed | tf_op | source)
XLA Modules:
  0.0 92.4 jit_solution(9325913373456014609)
XLA Ops:
  0.0 0.0 copy-start
  0.0 2.2 %copy-done = bf16[1024,2048]{1,0:T(8,128)(2,1)S(1)} copy-done((bf16[1024,2048]{1,0:T(8,128)(2,1)S(1)}, bf16[1024,2048]{1,0:T(8,128)(2,1)}, u32[]{:S(2)}) %copy-start) | copy-done | bytes 4194328
  2.2 0.0 copy-start.1
  2.2 1.0 %copy-done.1 = bf16[16,16,1024]{2,1,0:T(8,128)(2,1)S(1)} copy-done((bf16[16,16,1024]{2,1,0:T(8,128)(2,1)S(1)}, bf16[16,16,1024]{2,1,0:T(8,128)(2,1)}, u32[]{:S(2)}) %copy-start.1) | copy-done | bytes 524312
  3.2 0.0 copy-start.2
  3.2 0.9 %copy-done.2 = bf16[8,1,2,64,64]{4,3,2,1,0:T(8,128)(2,1)S(1)} copy-done((bf16[8,1,2,64,64]{4,3,2,1,0:T(8,128)(2,1)S(1)}, bf16[8,1,2,64,64]{4,3,2,1,0:T(8,128)(2,1)}, u32[]{:S(2)}) %copy-start.2) | copy-done | bytes 131096
  4.2 0.0 copy-start.3
  4.2 0.7 copy-done.3
  4.8 86.7 %forced_response.1 = bf16[16,16,1024]{2,1,0:T(8,128)(2,1)S(1)} custom-call(bf16[16,16,1024]{2,1,0:T(8,128)(2,1)S(1)} %copy-done.1, bf16[1024,2048]{1,0:T(8,128)(2,1)S(1)} %copy-done, bf16[8,2,64,64]{3,2,1,0:T(8,128)(2,1)S(1)} %bitcast.2, s32[1,128]{1,0:T(1,128)S(1)} %bitcast.3), custom_call_target="tpu_custom_call" | custom-call | tf_op jit(solution)/shard_map/forced_response/pallas_call | solution.py:375
  91.6 0.8 copy.6
Async XLA Ops:
  0.0 2.2 %copy-start = (bf16[1024,2048]{1,0:T(8,128)(2,1)S(1)}, bf16[1024,2048]{1,0:T(8,128)(2,1)}, u32[]{:S(2)}) copy-start(bf16[1024,2048]{1,0:T(8,128)(2,1)} %s_hbm.1) | copy-start | bytes 12582916
  2.2 1.0 %copy-start.1 = (bf16[16,16,1024]{2,1,0:T(8,128)(2,1)S(1)}, bf16[16,16,1024]{2,1,0:T(8,128)(2,1)}, u32[]{:S(2)}) copy-start(bf16[16,16,1024]{2,1,0:T(8,128)(2,1)} %f_hbm.1) | copy-start | bytes 1572868
  3.2 0.9 %copy-start.2 = (bf16[8,1,2,64,64]{4,3,2,1,0:T(8,128)(2,1)S(1)}, bf16[8,1,2,64,64]{4,3,2,1,0:T(8,128)(2,1)}, u32[]{:S(2)}) copy-start(bf16[8,1,2,64,64]{4,3,2,1,0:T(8,128)(2,1)} %param.6) | copy-start | bytes 393220
  4.2 0.7 copy-start.3

commit v2 on v1

v2 whole, which is shorter than its diff:
```python
import functools
import math

import jax
import jax.numpy as jnp
from jax import lax
from jax.experimental import pallas as pl
from jax.experimental.pallas import tpu as pltpu
from jax.sharding import PartitionSpec as P

BF16 = jnp.bfloat16
F32 = jnp.float32
MESH = pl.DeviceIdType.MESH

DIMS = dict(Z=8, X=4, H=2, Y=4)
LAG = 6


def kernel(
    Z, X, H, Y,
    f_hbm, s_hbm, inv_hbm, harm_hbm, out_hbm,
    f_v, s_v, inv_v, harm_v, pbuf, sendx, recvx, sendz, recvz, totz,
    t_hi, t_lo, u_hi, u_lo, fwd, bwd, amat, xg, rg, qacc, cacc, csend, coords, acc, out_v,
    f_sem, s_sem, i_sem, h_sem, o_sem, sa_sem, ra_sem,
    sx_sem, rx_sem, sz_sem, rz_sem, sg_sem, rg_sem, sr_sem, rr_sem,
    scz_sem, rcz_sem, scx_sem, rcx_sem,
):
    fam = inv_v.shape[2]
    slots = inv_v.shape[0]
    cases, own_t, depth = f_v.shape
    ct = cases * own_t
    half = ct // H
    group = Y * 2
    azis = H * group
    length = azis * own_t
    nh = harm_v.shape[1]
    ring = H * Z
    parts = 2 * H * slots
    own_cases = cases // H

    dof = lax.axis_index("dof")
    azi = lax.axis_index("azi")
    x = dof % X
    z = dof // X
    core = azi % 2
    y = (azi // 2) % Y
    h = azi // group
    place = h * Z + z

    def x_peer(r):
        return {"dof": z * X + (x + r) % X, "azi": azi}

    def ring_peer(r):
        there = (place + r) % ring
        return {"dof": (there % Z) * X + x, "azi": ((there // Z) * Y + y) * 2 + core}

    def y_peer(r):
        return {"dof": dof, "azi": (h * Y + (y + r) % Y) * 2 + core}

    def c_peer():
        return {"dof": dof, "azi": (h * Y + y) * 2 + 1 - core}

    peers = [ring_peer(r) for r in range(1, ring)] + [x_peer(r) for r in range(1, X)]
    peers += [y_peer(r) for r in range(1, Y)] + [c_peer()]

    barrier = pltpu.get_barrier_semaphore()
    for peer in peers:
        pl.semaphore_signal(barrier, inc=1, device_id=peer, device_id_type=MESH)

    def remote(src, dst, send, recv, peer):
        return pltpu.make_async_remote_copy(
            src_ref=src, dst_ref=dst, send_sem=send, recv_sem=recv,
            device_id=peer, device_id_type=MESH,
        )

    def offset(i):
        return jnp.where(i % 2 == 1, (i + 1) // 2, (Z - i // 2) % Z)

    def f_copy():
        return pltpu.make_async_copy(f_hbm, f_v, f_sem)

    def s_copy(o):
        target = (z + o) % Z
        columns = pl.ds(pl.multiple_of(target * (X * fam), X * fam), X * fam)
        return pltpu.make_async_copy(s_hbm.at[:, columns], s_v.at[o], s_sem.at[o])

    def i_copy():
        return pltpu.make_async_copy(inv_hbm, inv_v, i_sem)

    def h_copy():
        return pltpu.make_async_copy(harm_hbm, harm_v, h_sem)

    f_copy().start()
    for i in range(Z):
        s_copy(offset(i)).start()
    i_copy().start()
    h_copy().start()
    f_copy().wait()

    def x_copy(o, r):
        rows = pl.ds(pl.multiple_of(((x + r) % X) * fam, fam), fam)
        return remote(
            sendx.at[o, rows], recvx.at[o, r - 1], sx_sem.at[o, r - 1], rx_sem.at[o, r - 1], x_peer(r)
        )

    def multiply(o):
        s_copy(o).wait()
        part = jnp.dot(f_v[...].reshape(ct, depth), s_v[o], preferred_element_type=F32)
        part = part.T
        pbuf[o] = part
        sendx[o] = part.astype(BF16)

    multiply(0)

    i_copy().wait()
    for s in range(slots):
        amat[h, s * fam:(s + 1) * fam, 0:fam] = inv_v[s, 0]
        amat[h, s * fam:(s + 1) * fam, fam:2 * fam] = inv_v[s, 1]

    def a_copy(r):
        return remote(amat.at[h], amat.at[h], sa_sem.at[r - 1], ra_sem.at[r - 1], ring_peer(r * Z))

    def a_arrival(r):
        there = (h - r + H) % H
        return remote(amat.at[there], amat.at[there], sa_sem.at[r - 1], ra_sem.at[r - 1], ring_peer(r * Z))

    pl.semaphore_wait(barrier, len(peers))
    for r in range(1, H):
        a_copy(r).start()
    for r in range(1, X):
        x_copy(0, r).start()

    def multiply_send(i, carry):
        o = offset(i)
        multiply(o)
        for r in range(1, X):
            x_copy(o, r).start()
        return carry

    lax.fori_loop(1, Z, multiply_send, 0)

    own_rows = pl.ds(pl.multiple_of(x * fam, fam), fam)

    def z_copy(r):
        there = (place + r) % ring
        return remote(
            sendz.at[r % Z, there // Z], recvz.at[r], sz_sem.at[r], rz_sem.at[r], ring_peer(r)
        )

    def x_sum(o):
        total = pbuf[o, own_rows]
        for r in range(1, X):
            x_copy(o, r).wait_recv()
            total += recvx[o, r - 1].astype(F32)
        return total

    first = x_sum(0)
    for hh in range(H):
        piece = first[:, hh * half:(hh + 1) * half]
        sendz[0, hh] = piece.astype(BF16)
        totz[hh] = piece
    for k in range(1, H):
        z_copy(k * Z).start()
    kept = totz[h]
    totz[...] = jnp.zeros_like(totz)
    totz[h] = kept

    def x_reduce(i, carry):
        o = offset(i)
        total = x_sum(o)
        for hh in range(H):
            sendz[o, hh] = total[:, hh * half:(hh + 1) * half].astype(BF16)
        for k in range(H):
            z_copy(o + k * Z).start()
        return carry

    lax.fori_loop(1, Z, x_reduce, 0)

    h_copy().wait()
    lanes = (((1,), (1,)), ((), ()))
    table_shape = (length, ct)
    rows_t = lax.broadcasted_iota(jnp.int32, table_shape, 0)
    cols_t = lax.broadcasted_iota(jnp.int32, table_shape, 1)
    quarter = length // 4
    harm = harm_v[...].astype(F32).astype(BF16)

    def cosine(index):
        return jnp.cos((index % length).astype(F32) * (2.0 * math.pi / length))

    def split(value):
        high = value.astype(BF16)
        return high, (value - high.astype(F32)).astype(BF16)

    def slot_of(part, device):
        return (((part // slots) % H) * group + device) * slots + part % slots

    column = lax.broadcasted_iota(jnp.int32, (ct, nh), 0)
    lane = lax.broadcasted_iota(jnp.int32, (ct, nh), 1)
    pick = jnp.where(lane == slot_of(column % parts, y * 2 + core), 1.0, 0.0).astype(BF16)
    own_h = lax.dot_general(
        jnp.broadcast_to(harm, (length, nh)), pick, lanes, preferred_element_type=F32
    ).astype(jnp.int32)
    imag = (cols_t % parts) // (H * slots)
    t_hi[...], t_lo[...] = split(cosine(own_h * rows_t + imag * quarter))

    row_s = lax.broadcasted_iota(jnp.int32, (length, nh), 0)
    lane_s = lax.broadcasted_iota(jnp.int32, (length, nh), 1)
    pick_rows = jnp.where(lane_s == slot_of(row_s % parts, row_s // parts), 1.0, 0.0).astype(BF16)
    all_h = lax.dot_general(
        pick_rows, jnp.broadcast_to(harm, (ct, nh)), lanes, preferred_element_type=F32
    ).astype(jnp.int32)
    sample = ((cols_t // half) * group + y * 2 + core) * own_t + cols_t % own_t
    imag = (rows_t % parts) // (H * slots)
    weight = jnp.where(all_h == 0, 1.0 / length, 2.0 / length)
    u_hi[...], u_lo[...] = split(weight * cosine(all_h * sample + imag * quarter))

    row_c = lax.broadcasted_iota(jnp.int32, (ct, ct), 0)
    col_c = lax.broadcasted_iota(jnp.int32, (ct, ct), 1)
    same_fwd = jnp.where((row_c // own_t) % own_cases == col_c // parts, 1.0, 0.0).astype(BF16)
    same_bwd = jnp.where(row_c // parts == (col_c // own_t) % own_cases, 1.0, 0.0).astype(BF16)

    def owner(slot):
        return ((y - slot // 2 + Y) % Y) * 2 + (core + slot % 2) % 2

    def build_fwd(slot, carry):
        for n, ref in enumerate((t_hi, t_lo)):
            for hh in range(H):
                start = (hh * group + owner(slot)) * own_t
                block = ref[pl.ds(pl.multiple_of(start, own_t), own_t)]
                wide = jnp.broadcast_to(block[None], (own_cases, own_t, ct)).reshape(half, ct)
                fwd[slot, n, hh * half:(hh + 1) * half] = wide * same_fwd[hh * half:(hh + 1) * half]
        return carry

    def build_bwd(slot, carry):
        for n, ref in enumerate((u_hi, u_lo)):
            block = ref[pl.ds(pl.multiple_of(owner(slot) * parts, parts), parts)]
            wide = jnp.broadcast_to(block[None], (own_cases, parts, ct)).reshape(ct, ct)
            bwd[slot, n] = wide * same_bwd
        return carry

    lax.fori_loop(0, group, build_fwd, 0)

    def z_sum(r):
        z_copy(r).wait_recv()
        source = ((place - r + ring) % ring) // Z
        totz[source] += recvz[r].astype(F32)

    for k in range(1, H):
        z_sum(k * Z)

    def z_sums(i, carry):
        for k in range(H):
            z_sum(offset(i) + k * Z)
        return carry

    lax.fori_loop(1, Z, z_sums, 0)
    for hh in range(H):
        xg[0, :, hh * half:(hh + 1) * half] = totz[hh].astype(BF16)

    def gather(buf, send, recv, consume, between):
        def to_y(r):
            return remote(buf.at[0], buf.at[2 * r], send.at[2 * r], recv.at[2 * r], y_peer(r))

        def to_c(r):
            return remote(
                buf.at[2 * r], buf.at[2 * r + 1], send.at[2 * r + 1], recv.at[2 * r + 1], c_peer()
            )

        near = [1, 3, 2] if Y == 4 else list(range(1, Y))
        for r in near:
            to_y(r).start()
        to_c(0).start()
        between()
        consume(0)
        for r in near:
            to_y(r).wait_recv()
            to_c(r).start()
        to_c(0).wait_recv()
        consume(1)
        for r in near:
            consume(2 * r)
        for r in near:
            to_c(r).wait_recv()
            consume(2 * r + 1)
        for r in near:
            to_y(r).wait_send()
        for r in range(Y):
            to_c(r).wait_send()

    qacc[...] = jnp.zeros_like(qacc)

    def forward(slot):
        block = xg[slot]
        qacc[...] += (
            jnp.dot(block, fwd[slot, 0], preferred_element_type=F32)
            + jnp.dot(block, fwd[slot, 1], preferred_element_type=F32)
        )

    gather(xg, sg_sem, rg_sem, forward, lambda: lax.fori_loop(0, group, build_bwd, 0))

    for r in range(1, H):
        a_arrival(r).wait_recv()
    q = qacc[...]
    cols = lax.broadcasted_iota(jnp.int32, (fam, ct), 1)
    shift = H * slots
    turned = jnp.where((cols // shift) % 2 == 0, -pltpu.roll(q, ct - shift, 1), pltpu.roll(q, shift, 1))
    q_hi, q_lo = split(jnp.concatenate([q, turned], axis=0))
    response = jnp.zeros((fam, ct), F32)
    for hh in range(H):
        solved = jnp.dot(amat[hh], q_hi, preferred_element_type=F32)
        solved += jnp.dot(amat[hh], q_lo, preferred_element_type=F32)
        for s in range(slots):
            response = jnp.where(
                cols % shift == hh * slots + s, solved[s * fam:(s + 1) * fam], response
            )
    rg[0] = response.astype(BF16)

    cacc[...] = jnp.zeros_like(cacc)

    def backward(slot):
        block = rg[slot]
        cacc[...] += (
            jnp.dot(block, bwd[slot, 0], preferred_element_type=F32)
            + jnp.dot(block, bwd[slot, 1], preferred_element_type=F32)
        )

    gather(rg, sr_sem, rr_sem, backward, lambda: None)

    for hh in range(H):
        csend[hh] = cacc[:, hh * half:(hh + 1) * half].astype(BF16)
    coords[0, own_rows] = csend[h]

    def c_to_ring(r):
        there = (place + r) % ring
        return remote(
            csend.at[there // Z], coords.at[r, own_rows], scz_sem.at[r], rcz_sem.at[r], ring_peer(r)
        )

    def c_to_x(r, q):
        return remote(
            coords.at[r, own_rows], coords.at[r, own_rows],
            scx_sem.at[r, q - 1], rcx_sem.at[r, q - 1], x_peer(q),
        )

    def c_from_x(r, q):
        rows = pl.ds(pl.multiple_of(((x - q + X) % X) * fam, fam), fam)
        return remote(
            coords.at[r, rows], coords.at[r, rows],
            scx_sem.at[r, q - 1], rcx_sem.at[r, q - 1], x_peer(q),
        )

    def step(i):
        return jnp.where(i % 2 == 1, (i + 1) // 2, (ring - i // 2) % ring)

    for q in range(1, X):
        c_to_x(0, q).start()

    def send_ring(i, carry):
        c_to_ring(step(i)).start()
        return carry

    lax.fori_loop(1, ring, send_ring, 0)
    acc[...] = jnp.zeros_like(acc)

    def pass_on(i):
        r = step(i)
        c_to_ring(r).wait_recv()
        for q in range(1, X):
            c_to_x(r, q).start()

    def displace(i):
        r = step(i)
        for q in range(1, X):
            c_from_x(r, q).wait_recv()
        source = ((place - r + ring) % ring) // Z
        block = coords[r].astype(F32).T.astype(BF16)
        acc[source] += lax.dot_general(
            block, s_v[(Z - r % Z) % Z], lanes, preferred_element_type=F32
        )

    lag = min(LAG, ring)
    lax.fori_loop(1, lag, lambda i, c: (pass_on(i), c)[1], 0)
    lax.fori_loop(lag, ring, lambda i, c: (pass_on(i), displace(i - lag), c)[2], 0)
    lax.fori_loop(ring - lag, ring, lambda i, c: (displace(i), c)[1], 0)

    out_v[...] = acc[...].astype(BF16).reshape(cases, own_t, depth)
    out_copy = pltpu.make_async_copy(out_v, out_hbm, o_sem)
    out_copy.start()

    def drain_x(o, carry):
        for r in range(1, X):
            x_copy(o, r).wait_send()
        return carry

    def drain_ring(r, carry):
        z_copy(r).wait_send()
        c_to_ring(r).wait_send()
        return carry

    def drain_coords(r, carry):
        for q in range(1, X):
            c_to_x(r, q).wait_send()
        return carry

    lax.fori_loop(0, Z, drain_x, 0)
    lax.fori_loop(1, ring, drain_ring, 0)
    lax.fori_loop(0, ring, drain_coords, 0)
    for r in range(1, H):
        a_copy(r).wait_send()
    out_copy.wait()


def shards(dims, forcing, mode_shapes, inverses, harmonic_table):
    Z, X, H, Y = dims["Z"], dims["X"], dims["H"], dims["Y"]
    cases, own_t, depth = forcing.shape
    slots, _, _, fam, _ = inverses.shape
    ct = cases * own_t
    half = ct // H
    group = Y * 2
    length = H * group * own_t
    nh = harmonic_table.shape[0]
    ring = H * Z
    any_space = pl.BlockSpec(memory_space=pl.ANY)
    dma = pltpu.SemaphoreType.DMA
    xs, hs = max(X - 1, 1), max(H - 1, 1)
    return pl.pallas_call(
        functools.partial(kernel, Z, X, H, Y),
        out_shape=jax.ShapeDtypeStruct(forcing.shape, BF16),
        in_specs=[any_space] * 4,
        out_specs=any_space,
        scratch_shapes=[
            pltpu.VMEM((cases, own_t, depth), BF16),
            pltpu.VMEM((Z, depth, X * fam), BF16),
            pltpu.VMEM((slots, 2, fam, fam), BF16),
            pltpu.VMEM((1, nh), jnp.int32),
            pltpu.VMEM((Z, X * fam, ct), F32),
            pltpu.VMEM((Z, X * fam, ct), BF16),
            pltpu.VMEM((Z, xs, fam, ct), BF16),
            pltpu.VMEM((Z, H, fam, half), BF16),
            pltpu.VMEM((ring, fam, half), BF16),
            pltpu.VMEM((H, fam, half), F32),
            pltpu.VMEM((length, ct), BF16),
            pltpu.VMEM((length, ct), BF16),
            pltpu.VMEM((length, ct), BF16),
            pltpu.VMEM((length, ct), BF16),
            pltpu.VMEM((group, 2, ct, ct), BF16),
            pltpu.VMEM((group, 2, ct, ct), BF16),
            pltpu.VMEM((H, slots * fam, 2 * fam), BF16),
            pltpu.VMEM((group, fam, ct), BF16),
            pltpu.VMEM((group, fam, ct), BF16),
            pltpu.VMEM((fam, ct), F32),
            pltpu.VMEM((fam, ct), F32),
            pltpu.VMEM((H, fam, half), BF16),
            pltpu.VMEM((ring, X * fam, half), BF16),
            pltpu.VMEM((H, half, depth), F32),
            pltpu.VMEM((cases, own_t, depth), BF16),
            dma, dma((Z,)), dma, dma, dma, dma((hs,)), dma((hs,)),
            dma((Z, xs)), dma((Z, xs)), dma((ring,)), dma((ring,)),
            dma((group,)), dma((group,)), dma((group,)), dma((group,)),
            dma((ring,)), dma((ring,)), dma((ring, xs)), dma((ring, xs)),
        ],
        compiler_params=pltpu.CompilerParams(
            collective_id=0, has_side_effects=True, vmem_limit_bytes=60 * 1024 * 1024
        ),
        name="forced_response",
    )(
        forcing,
        mode_shapes,
        inverses.reshape(slots, 2, fam, fam),
        harmonic_table.reshape(1, nh),
    )


def solution(mesh, dims=DIMS):
    in_specs = (P(None, "azi", "dof"), P("dof", None), P("azi", "dof", None, None, None), P())
    out_specs = P(None, "azi", "dof")
    return jax.shard_map(
        functools.partial(shards, dims), mesh=mesh, in_specs=in_specs, out_specs=out_specs, check_vma=False
    )
```

time: 94.1 us -> 79.6 us (0.85)
  the two profiles are of different devices: /device:TPU:6 before, /device:TPU:32 now
where the time goes in v2:
time: 79.6 us; the launch traced here: 79.5 us
  Pallas kernels  77.6 us (97%)
  local copies, waits for them, and re-layouts  1.88 us (2%)
    pallas_call x1, Pallas kernels, shards(): pl.pallas_call(functools.partial(kernel, Z, X, H, Y), out_shape=jax.Shape...  77.6 us
    unnamed x1, local copies, waits for them, and re-layouts  1.88 us

profile of v2, /device:TPU:32, one launch (start us, length us, event | category | flops | bytes accessed | tf_op | source)
XLA Modules:
  0.0 79.5 jit_solution(14886447553295367291)
XLA Ops:
  0.0 77.6 %forced_response.1 = bf16[16,16,1024]{2,1,0:T(8,128)(2,1)} custom-call(bf16[16,16,1024]{2,1,0:T(8,128)(2,1)} %f_hbm.1, bf16[1024,2048]{1,0:T(8,128)(2,1)} %s_hbm.1, bf16[8,2,64,64]{3,2,1,0:T(8,128)(2,1)} %bitcast.2, s32[1,128]{1,0:T(1,128)} %bitcast.3), custom_call_target="tpu_custom_call" | custom-call | tf_op jit(solution)/shard_map/forced_response/pallas_call | solution.py:426
  77.6 1.9 %copy.6 = bf16[16,16,1024]{2,1,0:T(8,128)(2,1)} copy(bf16[16,16,1024]{2,1,0:T(8,128)(2,1)} %forced_response.1) | data formatting | bytes 1048576

commit v3 on v2

--- a/solution.py
+++ b/solution.py
@@ -13,14 +13,16 @@
 MESH = pl.DeviceIdType.MESH
 
 DIMS = dict(Z=8, X=4, H=2, Y=4)
-LAG = 6
+RUN = 4
+INV_PIECES = 4
+INV_EARLY = 2
 
 
 def kernel(
     Z, X, H, Y,
     f_hbm, s_hbm, inv_hbm, harm_hbm, out_hbm,
     f_v, s_v, inv_v, harm_v, pbuf, sendx, recvx, sendz, recvz, totz,
-    t_hi, t_lo, u_hi, u_lo, fwd, bwd, amat, xg, rg, qacc, cacc, csend, coords, acc, out_v,
+    t_hi, t_lo, u_hi, u_lo, fwd, bwd, asend, amat, xg, rg, qacc, cacc, csend, coords, acc, out_v,
     f_sem, s_sem, i_sem, h_sem, o_sem, sa_sem, ra_sem,
     sx_sem, rx_sem, sz_sem, rz_sem, sg_sem, rg_sem, sr_sem, rr_sem,
     scz_sem, rcz_sem, scx_sem, rcx_sem,
@@ -37,6 +39,7 @@
     ring = H * Z
     parts = 2 * H * slots
     own_cases = cases // H
+    away = Z // 2 if H > 1 else 0
 
     dof = lax.axis_index("dof")
     azi = lax.axis_index("azi")
@@ -80,7 +83,7 @@
         return pltpu.make_async_copy(f_hbm, f_v, f_sem)
 
     def s_copy(o):
-        target = (z + o) % Z
+        target = (z + o + away) % Z
         columns = pl.ds(pl.multiple_of(target * (X * fam), X * fam), X * fam)
         return pltpu.make_async_copy(s_hbm.at[:, columns], s_v.at[o], s_sem.at[o])
 
@@ -114,19 +117,31 @@
 
     i_copy().wait()
     for s in range(slots):
-        amat[h, s * fam:(s + 1) * fam, 0:fam] = inv_v[s, 0]
-        amat[h, s * fam:(s + 1) * fam, fam:2 * fam] = inv_v[s, 1]
-
-    def a_copy(r):
-        return remote(amat.at[h], amat.at[h], sa_sem.at[r - 1], ra_sem.at[r - 1], ring_peer(r * Z))
-
-    def a_arrival(r):
-        there = (h - r + H) % H
-        return remote(amat.at[there], amat.at[there], sa_sem.at[r - 1], ra_sem.at[r - 1], ring_peer(r * Z))
+        asend[s * fam:(s + 1) * fam, 0:fam] = inv_v[s, 0]
+        asend[s * fam:(s + 1) * fam, fam:2 * fam] = inv_v[s, 1]
+    inv_rows = slots * fam // INV_PIECES
+    inv_ways = [(away + k * Z) % ring for k in range(H)]
+
+    def a_piece(k, n, there):
+        rows = slice(n * inv_rows, (n + 1) * inv_rows)
+        return remote(
+            asend.at[rows], amat.at[there, rows], sa_sem.at[k, n], ra_sem.at[k, n], ring_peer(inv_ways[k])
+        )
+
+    def a_copy(k, n):
+        return a_piece(k, n, h)
+
+    def a_arrival(k, n):
+        return a_piece(k, n, ((place - inv_ways[k] + ring) % ring) // Z)
+
+    if away == 0:
+        amat[h] = asend[...]
+    sent_inverses = [(k, n) for n in range(INV_PIECES) for k in range(H) if inv_ways[k] != 0]
+    early = [(k, n) for k, n in sent_inverses if n < INV_EARLY]
 
     pl.semaphore_wait(barrier, len(peers))
-    for r in range(1, H):
-        a_copy(r).start()
+    for k, n in early:
+        a_copy(k, n).start()
     for r in range(1, X):
         x_copy(0, r).start()
 
@@ -175,6 +190,8 @@
         return carry
 
     lax.fori_loop(1, Z, x_reduce, 0)
+    for k, n in sent_inverses[len(early):]:
+        a_copy(k, n).start()
 
     h_copy().wait()
     lanes = (((1,), (1,)), ((), ()))
@@ -298,8 +315,8 @@
 
     gather(xg, sg_sem, rg_sem, forward, lambda: lax.fori_loop(0, group, build_bwd, 0))
 
-    for r in range(1, H):
-        a_arrival(r).wait_recv()
+    for k, n in sent_inverses:
+        a_arrival(k, n).wait_recv()
     q = qacc[...]
     cols = lax.broadcasted_iota(jnp.int32, (fam, ct), 1)
     shift = H * slots
@@ -326,62 +343,90 @@
 
     gather(rg, sr_sem, rr_sem, backward, lambda: None)
 
+    run = min(RUN, Z)
+    runs = ring // run
+    own_run, position = place // run, place % run
     for hh in range(H):
         csend[hh] = cacc[:, hh * half:(hh + 1) * half].astype(BF16)
     coords[0, own_rows] = csend[h]
 
-    def c_to_ring(r):
-        there = (place + r) % ring
-        return remote(
-            csend.at[there // Z], coords.at[r, own_rows], scz_sem.at[r], rcz_sem.at[r], ring_peer(r)
-        )
-
-    def c_to_x(r, q):
-        return remote(
-            coords.at[r, own_rows], coords.at[r, own_rows],
-            scx_sem.at[r, q - 1], rcx_sem.at[r, q - 1], x_peer(q),
-        )
-
-    def c_from_x(r, q):
+    def place_peer(there):
+        return {"dof": (there % Z) * X + x, "azi": ((there // Z) * Y + y) * 2 + core}
+
+    def c_to_run(d):
+        there = ((own_run + d) % runs) * run + position
+        slot = d * run
+        return remote(
+            csend.at[there // Z], coords.at[slot, own_rows], scz_sem.at[slot], rcz_sem.at[slot],
+            place_peer(there),
+        )
+
+    def c_in_run(d, n):
+        slot = d * run + n
+        return remote(
+            coords.at[d * run, own_rows], coords.at[slot, own_rows], scz_sem.at[slot], rcz_sem.at[slot],
+            place_peer(own_run * run + (position + n) % run),
+        )
+
+    def c_to_x(slot, q):
+        return remote(
+            coords.at[slot, own_rows], coords.at[slot, own_rows],
+            scx_sem.at[slot, q - 1], rcx_sem.at[slot, q - 1], x_peer(q),
+        )
+
+    def c_from_x(slot, q):
         rows = pl.ds(pl.multiple_of(((x - q + X) % X) * fam, fam), fam)
         return remote(
-            coords.at[r, rows], coords.at[r, rows],
-            scx_sem.at[r, q - 1], rcx_sem.at[r, q - 1], x_peer(q),
-        )
-
-    def step(i):
-        return jnp.where(i % 2 == 1, (i + 1) // 2, (ring - i // 2) % ring)
-
-    for q in range(1, X):
-        c_to_x(0, q).start()
-
-    def send_ring(i, carry):
-        c_to_ring(step(i)).start()
-        return carry
-
-    lax.fori_loop(1, ring, send_ring, 0)
+            coords.at[slot, rows], coords.at[slot, rows],
+            scx_sem.at[slot, q - 1], rcx_sem.at[slot, q - 1], x_peer(q),
+        )
+
+    def along_x(slot):
+        for q in range(1, X):
+            c_to_x(slot, q).start()
+
+    def along_run(d):
+        for n in range(1, run):
+            c_in_run(d, n).start()
+
+    def displace(n):
+        k = n // run
+        d = jnp.where(k % 2 == 1, (k + 1) // 2, (runs - k // 2) % runs)
+        slot = d * run + n % run
+        for q in range(1, X):
+            c_from_x(slot, q).wait_recv()
+        source = ((own_run - d + runs) % runs) * run + (position - n % run + run) % run
+        block = coords[slot].astype(F32).T.astype(BF16)
+        acc[source // Z] += lax.dot_general(
+            block, s_v[(source % Z - z + Z) % Z], lanes, preferred_element_type=F32
+        )
+
+    def displace_all(low, high):
+        if low < high:
+            lax.fori_loop(low, high, lambda n, c: (displace(n), c)[1], 0)
+
+    far = sorted(range(1, runs), key=lambda d: min(d, runs - d))
+    for d in far[::-1]:
+        c_to_run(d).start()
+    along_run(0)
+    along_x(0)
     acc[...] = jnp.zeros_like(acc)
-
-    def pass_on(i):
-        r = step(i)
-        c_to_ring(r).wait_recv()
-        for q in range(1, X):
-            c_to_x(r, q).start()
-
-    def displace(i):
-        r = step(i)
-        for q in range(1, X):
-            c_from_x(r, q).wait_recv()
-        source = ((place - r + ring) % ring) // Z
-        block = coords[r].astype(F32).T.astype(BF16)
-        acc[source] += lax.dot_general(
-            block, s_v[(Z - r % Z) % Z], lanes, preferred_element_type=F32
-        )
-
-    lag = min(LAG, ring)
-    lax.fori_loop(1, lag, lambda i, c: (pass_on(i), c)[1], 0)
-    lax.fori_loop(lag, ring, lambda i, c: (pass_on(i), displace(i - lag), c)[2], 0)
-    lax.fori_loop(ring - lag, ring, lambda i, c: (displace(i), c)[1], 0)
+    for n in range(1, run):
+        c_in_run(0, n).wait_recv()
+        along_x(n)
+    done = 0
+    for d in far:
+        c_to_run(d).wait_recv()
+        along_run(d)
+        along_x(d * run)
+        if d == far[-1]:
+            displace_all(0, 1)
+            done = 1
+    for d in far:
+        for n in range(1, run):
+            c_in_run(d, n).wait_recv()
+            along_x(d * run + n)
+    displace_all(done, ring)
 
     out_v[...] = acc[...].astype(BF16).reshape(cases, own_t, depth)
     out_copy = pltpu.make_async_copy(out_v, out_hbm, o_sem)
@@ -394,7 +439,6 @@
 
     def drain_ring(r, carry):
         z_copy(r).wait_send()
-        c_to_ring(r).wait_send()
         return carry
 
     def drain_coords(r, carry):
@@ -405,8 +449,13 @@
     lax.fori_loop(0, Z, drain_x, 0)
     lax.fori_loop(1, ring, drain_ring, 0)
     lax.fori_loop(0, ring, drain_coords, 0)
-    for r in range(1, H):
-        a_copy(r).wait_send()
+    for d in far:
+        c_to_run(d).wait_send()
+    for d in range(runs):
+        for n in range(1, run):
+            c_in_run(d, n).wait_send()
+    for k, n in sent_inverses:
+        a_copy(k, n).wait_send()
     out_copy.wait()
 
 
@@ -422,7 +471,7 @@
     ring = H * Z
     any_space = pl.BlockSpec(memory_space=pl.ANY)
     dma = pltpu.SemaphoreType.DMA
-    xs, hs = max(X - 1, 1), max(H - 1, 1)
+    xs = max(X - 1, 1)
     return pl.pallas_call(
         functools.partial(kernel, Z, X, H, Y),
         out_shape=jax.ShapeDtypeStruct(forcing.shape, BF16),
@@ -445,6 +494,7 @@
             pltpu.VMEM((length, ct), BF16),
             pltpu.VMEM((group, 2, ct, ct), BF16),
             pltpu.VMEM((group, 2, ct, ct), BF16),
+            pltpu.VMEM((slots * fam, 2 * fam), BF16),
             pltpu.VMEM((H, slots * fam, 2 * fam), BF16),
             pltpu.VMEM((group, fam, ct), BF16),
             pltpu.VMEM((group, fam, ct), BF16),
@@ -454,7 +504,7 @@
             pltpu.VMEM((ring, X * fam, half), BF16),
             pltpu.VMEM((H, half, depth), F32),
             pltpu.VMEM((cases, own_t, depth), BF16),
-            dma, dma((Z,)), dma, dma, dma, dma((hs,)), dma((hs,)),
+            dma, dma((Z,)), dma, dma, dma, dma((H, INV_PIECES)), dma((H, INV_PIECES)),
             dma((Z, xs)), dma((Z, xs)), dma((ring,)), dma((ring,)),
             dma((group,)), dma((group,)), dma((group,)), dma((group,)),
             dma((ring,)), dma((ring,)), dma((ring, xs)), dma((ring, xs)),

time: 79.6 us -> 73.8 us (0.927)
  the two profiles are of different devices: /device:TPU:32 before, /device:TPU:6 now
where the time goes in v3:
time: 73.8 us; the launch traced here: 73.4 us
  Pallas kernels  71.5 us (97%)
  local copies, waits for them, and re-layouts  1.88 us (3%)
    pallas_call x1, Pallas kernels, shards(): pl.pallas_call(functools.partial(kernel, Z, X, H, Y), out_shape=jax.Shape...  71.5 us
    unnamed x1, local copies, waits for them, and re-layouts  1.88 us

profile of v3, /device:TPU:6, one launch (start us, length us, event | category | flops | bytes accessed | tf_op | source)
XLA Modules:
  0.0 73.4 jit_solution(12247062093624508391)
XLA Ops:
  0.0 71.5 %forced_response.1 = bf16[16,16,1024]{2,1,0:T(8,128)(2,1)} custom-call(bf16[16,16,1024]{2,1,0:T(8,128)(2,1)} %f_hbm.1, bf16[1024,2048]{1,0:T(8,128)(2,1)} %s_hbm.1, bf16[8,2,64,64]{3,2,1,0:T(8,128)(2,1)} %bitcast.2, s32[1,128]{1,0:T(1,128)} %bitcast.3), custom_call_target="tpu_custom_call" | custom-call | tf_op jit(solution)/shard_map/forced_response/pallas_call | solution.py:475
  71.5 1.9 %copy.6 = bf16[16,16,1024]{2,1,0:T(8,128)(2,1)} copy(bf16[16,16,1024]{2,1,0:T(8,128)(2,1)} %forced_response.1) | data formatting | bytes 1048576

commit v4 on v3

--- a/solution.py
+++ b/solution.py
@@ -50,6 +50,8 @@
     h = azi // group
     place = h * Z + z
 
+    far_x = sorted(range(1, X), key=lambda r: -min(r, X - r))
+
     def x_peer(r):
         return {"dof": z * X + (x + r) % X, "azi": azi}
 
@@ -148,7 +150,7 @@
     def multiply_send(i, carry):
         o = offset(i)
         multiply(o)
-        for r in range(1, X):
+        for r in far_x:
             x_copy(o, r).start()
         return carry
 
@@ -315,21 +317,26 @@
 
     gather(xg, sg_sem, rg_sem, forward, lambda: lax.fori_loop(0, group, build_bwd, 0))
 
-    for k, n in sent_inverses:
-        a_arrival(k, n).wait_recv()
     q = qacc[...]
     cols = lax.broadcasted_iota(jnp.int32, (fam, ct), 1)
     shift = H * slots
     turned = jnp.where((cols // shift) % 2 == 0, -pltpu.roll(q, ct - shift, 1), pltpu.roll(q, shift, 1))
     q_hi, q_lo = split(jnp.concatenate([q, turned], axis=0))
     response = jnp.zeros((fam, ct), F32)
-    for hh in range(H):
-        solved = jnp.dot(amat[hh], q_hi, preferred_element_type=F32)
-        solved += jnp.dot(amat[hh], q_lo, preferred_element_type=F32)
-        for s in range(slots):
-            response = jnp.where(
-                cols % shift == hh * slots + s, solved[s * fam:(s + 1) * fam], response
-            )
+    piece_slots = slots // INV_PIECES
+    for n in range(INV_PIECES):
+        for k, piece in sent_inverses:
+            if piece == n:
+                a_arrival(k, piece).wait_recv()
+        for hh in range(H):
+            block = amat[hh, n * inv_rows:(n + 1) * inv_rows]
+            solved = jnp.dot(block, q_hi, preferred_element_type=F32)
+            solved += jnp.dot(block, q_lo, preferred_element_type=F32)
+            for s in range(piece_slots):
+                response = jnp.where(
+                    cols % shift == hh * slots + n * piece_slots + s,
+                    solved[s * fam:(s + 1) * fam], response,
+                )
     rg[0] = response.astype(BF16)
 
     cacc[...] = jnp.zeros_like(cacc)
@@ -382,7 +389,7 @@
         )
 
     def along_x(slot):
-        for q in range(1, X):
+        for q in far_x:
             c_to_x(slot, q).start()
 
     def along_run(d):

time: 73.8 us -> 73.9 us (level)
  no operation moved by 1% of the time
where the time goes in v4:
time: 73.9 us; the launch traced here: 73.8 us
  Pallas kernels  71.9 us (97%)
  local copies, waits for them, and re-layouts  1.88 us (3%)
    pallas_call x1, Pallas kernels, shards(): pl.pallas_call(functools.partial(kernel, Z, X, H, Y), out_shape=jax.Shape...  71.9 us
    unnamed x1, local copies, waits for them, and re-layouts  1.88 us

profile of v4, /device:TPU:6, one launch (start us, length us, event | category | flops | bytes accessed | tf_op | source)
XLA Modules:
  0.0 73.8 jit_solution(857701749475046331)
XLA Ops:
  0.0 71.9 %forced_response.1 = bf16[16,16,1024]{2,1,0:T(8,128)(2,1)} custom-call(bf16[16,16,1024]{2,1,0:T(8,128)(2,1)} %f_hbm.1, bf16[1024,2048]{1,0:T(8,128)(2,1)} %s_hbm.1, bf16[8,2,64,64]{3,2,1,0:T(8,128)(2,1)} %bitcast.2, s32[1,128]{1,0:T(1,128)} %bitcast.3), custom_call_target="tpu_custom_call" | custom-call | tf_op jit(solution)/shard_map/forced_response/pallas_call | solution.py:482
  71.9 1.9 %copy.6 = bf16[16,16,1024]{2,1,0:T(8,128)(2,1)} copy(bf16[16,16,1024]{2,1,0:T(8,128)(2,1)} %forced_response.1) | data formatting | bytes 1048576
